TPU v7x, 32 devices: a whole 2x2x4 slice. The times are simulated.
32 devices in a mesh: ctx: 8 (over z, x), wa: 4 (over y, core).
Axes of the slice: x: 2, y: 2, z: 4, core: 2. Of those that a mesh axis runs over, the one named last changes fastest.
Arguments:
- x_in: bfloat16 [4, 1024, 1024], P('wa', 'ctx'), may hold values from -6 to 6
- seg_ids: int32 [4, 1024], P('wa'), may hold values from 0 to 2, never falling along the last dimension, each value on 1 to 512 neighbouring positions
- d_out: bfloat16 [4, 1024, 1024], P('wa', 'ctx'), may hold values from -6 to 6
- gain_in: float32 [1024], replicated, may hold values from 0.5 to 1.5
- w_mix_in: bfloat16 [1024, 4120], P(None, 'wa'), may hold values from -0.30078125 to 0.30078125
- conv_w: float32 [4, 1792], replicated, may hold values from -3 to 3
- conv_b: float32 [1792], replicated, may hold values from -3 to 3
- dt_bias: float32 [24], replicated, may hold values from -3 to 1
- a_log: float32 [24], replicated, may hold values from -8 to 0
- d_skip: float32 [24], replicated, may hold values from 0.5 to 1.5
- gain_gate: float32 [1536], replicated, may hold values from 0.5 to 1.5
- w_mix_out: bfloat16 [2048, 1024], P(None, 'wa'), may hold values from -0.25 to 0.25
- gain_ff: float32 [1024], replicated, may hold values from 0.5 to 1.5
- w_gate_up: bfloat16 [1024, 4096], P(None, 'wa'), may hold values from -0.1875 to 0.1875
- w_down: bfloat16 [2048, 1024], P(None, 'wa'), may hold values from -0.1875 to 0.1875
Outputs:
- out_rows: bfloat16 [4, 1024, 1024], P('wa', 'ctx')
- x_grad: float32 [4, 1024, 1024], P('wa', 'ctx')
- gain_in_grad: float32 [1024], replicated
- w_mix_in_grad: float32 [1024, 4120], P('ctx', 'wa')
- conv_w_grad: float32 [4, 1792], replicated
- conv_b_grad: float32 [1792], replicated
- dt_bias_grad: float32 [24], replicated
- a_log_grad: float32 [24], replicated
- d_skip_grad: float32 [24], replicated
- gain_gate_grad: float32 [1536], replicated
- w_mix_out_grad: float32 [2048, 1024], P('ctx', 'wa')
- gain_ff_grad: float32 [1024], replicated
- w_gate_up_grad: float32 [1024, 4096], P('ctx', 'wa')
- w_down_grad: float32 [2048, 1024], P('ctx', 'wa')
Inputs may be any that keep to these rules, and one draw needn't show every extreme that they name: `seg_ids`: in each stream the document numbers never fall, every document 0 to 2 is present with 1 to 512 positions, and one has exactly 512.
All inputs are finite; a program needn't handle non-finite values.
Results may differ from a plain program's by a relative error of at most 0.03.
Values may be sent and summed in bfloat16 or wider, within the bound.
A program may use at most 256 MiB of HBM per device.

v0:
```python
from functools import partial

import jax
import jax.numpy as jnp
from jax import lax
from jax.sharding import PartitionSpec as P

QHEADS = 8
KVHEADS = 2
HEAD_DIM = 64


EPS = 1e-05
ROPE_BASE = 100000000000.0
HIGH = lax.Precision.HIGHEST
KEY_BLOCK = 512


def prefix(shard, axis, combine, identity, reverse):
    length, position = (lax.axis_size(axis), lax.axis_index(axis))
    everything = jax.tree.map(lambda part: lax.all_gather(part, axis), shard)
    start = jax.tree.map(
        lambda part, zero: jnp.broadcast_to(jnp.asarray(zero, part.dtype), part.shape),
        shard,
        identity,
    )

    def lap(k, before):
        at = length - 1 - k if reverse else k
        reached = at > position if reverse else at < position
        new = combine(before, jax.tree.map(lambda part: part[at], everything))
        return jax.tree.map(lambda a, b: jnp.where(reached, a, b), new, before)

    return lax.fori_loop(0, length, lap, start)


def extended_2(cells, sides, width):
    for axis, dim in sides:
        count = lax.axis_size(axis)
        ends = count - 1
        head = lax.slice_in_dim(cells, 0, width, axis=dim)
        tail = lax.slice_in_dim(cells, cells.shape[dim] - width, cells.shape[dim], axis=dim)
        cells = jnp.concatenate(
            [
                lax.ppermute(tail, axis, [(i, (i + 1) % count) for i in range(ends)]),
                cells,
                lax.ppermute(head, axis, [((i + 1) % count, i) for i in range(ends)]),
            ],
            axis=dim,
        )
    return cells


def norm_rows(values, gain):
    return values * lax.rsqrt(jnp.mean(values * values, axis=-1, keepdims=True) + EPS) * gain


def swiglu(mixed):
    half_size = mixed.shape[-1] // 2
    return jax.nn.silu(mixed[:, :half_size]) * mixed[:, half_size:]


def rotate(values, positions, direction):
    head_size = values.shape[-1]
    half_size = head_size // 2
    frequency = ROPE_BASE ** (-2.0 * jnp.arange(half_size, dtype=jnp.float32) / head_size)
    angles = positions.astype(jnp.float32)[:, None] * frequency[None, :]
    cosine = jnp.cos(angles)[:, None, :]
    sine_part = direction * jnp.sin(angles)[:, None, :]
    first_half = values[..., :half_size]
    second_half = values[..., half_size:]
    return jnp.concatenate(
        [
            first_half * cosine - second_half * sine_part,
            second_half * cosine + first_half * sine_part,
        ],
        axis=-1,
    )


def conv_rows(extended, seg_ext, conv_w, conv_b):
    conv_lag = conv_w.shape[0] - 1
    length = extended.shape[0] - conv_lag
    summed = jnp.zeros((length, extended.shape[1]), jnp.float32) + conv_b[None, :]
    for tap_index in range(conv_lag + 1):
        same_doc = (seg_ext[tap_index : tap_index + length] == seg_ext[conv_lag:]).astype(
            jnp.float32
        )
        summed = (
            summed
            + conv_w[tap_index][None, :]
            * extended[tap_index : tap_index + length]
            * same_doc[:, None]
        )
    return jax.nn.silu(summed)


def block_inputs(extended, seg_ext, raw_dt, conv_w, conv_b, dt_bias, a_log, inner_width):
    mixed = conv_rows(extended, seg_ext, conv_w, conv_b)
    length = mixed.shape[0]
    mamba_heads = dt_bias.shape[0]
    state_size = (mixed.shape[1] - inner_width) // 2
    inputs_x = mixed[:, :inner_width].reshape(length, mamba_heads, inner_width // mamba_heads)
    b_rows = mixed[:, inner_width : inner_width + state_size]
    c_rows = mixed[:, inner_width + state_size :]
    step_dt = jax.nn.softplus(raw_dt + dt_bias[None, :])
    log_decay = -step_dt * jnp.exp(a_log)[None, :]
    return (inputs_x, b_rows, c_rows, step_dt, log_decay)


def block_state(inputs_x, b_rows, step_dt, log_decay, seg_block, seg_before):
    cumulative = jnp.cumsum(log_decay, axis=0)
    keep_end = (seg_block == seg_block[-1]).astype(jnp.float32)
    weights = jnp.exp(cumulative[-1][None, :] - cumulative) * keep_end[:, None] * step_dt
    end_state = jnp.einsum("shp,sn->hpn", weights[:, :, None] * inputs_x, b_rows, precision=HIGH)
    decay_all = jnp.exp(cumulative[-1]) * (seg_block[-1] == seg_before).astype(jnp.float32)
    return (decay_all, end_state)


def block_output(
    inputs_x, b_rows, c_rows, step_dt, log_decay, d_skip, seg_block, seg_before, state_in
):
    length = inputs_x.shape[0]
    cumulative = jnp.cumsum(log_decay, axis=0)
    lower_tri = jnp.arange(length)[:, None] >= jnp.arange(length)[None, :]
    allowed = lower_tri & (seg_block[:, None] == seg_block[None, :])
    across = cumulative.T
    exponent = jnp.where(allowed[None], across[:, :, None] - across[:, None, :], -jnp.inf)
    intersection = jnp.dot(c_rows, b_rows.T, precision=HIGH)
    mixing = jnp.exp(exponent) * intersection[None] * step_dt.T[:, None, :]
    inner_out = jnp.einsum("hts,shp->thp", mixing, inputs_x, precision=HIGH)
    carried = (seg_block == seg_before).astype(jnp.float32)
    from_state = (
        jnp.einsum("tn,hpn->thp", c_rows, state_in, precision=HIGH)
        * (jnp.exp(cumulative) * carried[:, None])[:, :, None]
    )
    return inner_out + from_state + d_skip[None, :, None] * inputs_x


def gated_norm(outputs, gate_rows, gain_gate):
    return norm_rows(outputs * jax.nn.silu(gate_rows), gain_gate)


def state_piece(seg_ext, seg_before, inner_width, extended, raw_dt, conv_w, conv_b, dt_bias, a_log):
    conv_lag = conv_w.shape[0] - 1
    inputs_x, b_rows, c_rows, step_dt, log_decay = block_inputs(
        extended, seg_ext, raw_dt, conv_w, conv_b, dt_bias, a_log, inner_width
    )
    return block_state(inputs_x, b_rows, step_dt, log_decay, seg_ext[conv_lag:], seg_before)


def out_piece(
    seg_ext,
    seg_before,
    inner_width,
    extended,
    raw_dt,
    gate_rows,
    conv_w,
    conv_b,
    dt_bias,
    a_log,
    d_skip,
    gain_gate,
    state_in,
):
    conv_lag = conv_w.shape[0] - 1
    inputs_x, b_rows, c_rows, step_dt, log_decay = block_inputs(
        extended, seg_ext, raw_dt, conv_w, conv_b, dt_bias, a_log, inner_width
    )
    outputs = block_output(
        inputs_x,
        b_rows,
        c_rows,
        step_dt,
        log_decay,
        d_skip,
        seg_ext[conv_lag:],
        seg_before,
        state_in,
    )
    return gated_norm(outputs.reshape(outputs.shape[0], inner_width), gate_rows, gain_gate)


def combine(earlier, later):
    return (earlier[0] * later[0], later[0][:, None, None] * earlier[1] + later[1])


def state_chain(lead, trailing):
    at_end = lax.axis_index("ctx") == lax.axis_size("ctx") - 1
    identity = (jnp.ones_like(lead[0]), jnp.zeros_like(lead[1]))
    before = prefix(lead, "ctx", combine, identity, False)
    through = combine(before, lead)
    joined = combine(through, trailing)
    handed = (jnp.where(at_end, joined[0], trailing[0]), jnp.where(at_end, joined[1], trailing[1]))
    after = prefix(handed, "ctx", combine, identity, True)
    return (before[1], jnp.where(at_end, through[1], after[1]))


def to_natural(stored, ctx_count):
    block_len = stored.shape[0] // (2 * ctx_count)
    tail_shape = stored.shape[1:]
    shaped = stored.reshape((ctx_count, 2, block_len) + tail_shape)
    return jnp.concatenate(
        [
            shaped[:, 0].reshape((ctx_count * block_len,) + tail_shape),
            shaped[::-1, 1].reshape((ctx_count * block_len,) + tail_shape),
        ],
        axis=0,
    )


def to_stored(natural, ctx_count):
    tail_shape = natural.shape[1:]
    half_len = natural.shape[0] // 2
    block_len = half_len // ctx_count
    leading = natural[:half_len].reshape((ctx_count, block_len) + tail_shape)
    trailing = natural[half_len:].reshape((ctx_count, block_len) + tail_shape)[::-1]
    return jnp.stack([leading, trailing], axis=1).reshape(natural.shape)


def key_bounds(seg_all, first_row, block_len, key_block):
    first_doc = jnp.take(seg_all, first_row)
    doc_start = jnp.sum((seg_all < first_doc).astype(jnp.int32))
    return (doc_start // key_block, (first_row + block_len - 1) // key_block + 1)


def block_scores(q_block, keys, seg_all, first_row, key_index, key_block, score_scale):
    key_start = key_index * key_block
    key_rows = lax.dynamic_slice_in_dim(keys, key_start, key_block, 0)
    seg_keys = lax.dynamic_slice_in_dim(seg_all, key_start, key_block, 0)
    seg_query = lax.dynamic_slice_in_dim(seg_all, first_row, q_block.shape[0], 0)
    query_pos = first_row + jnp.arange(q_block.shape[0], dtype=jnp.int32)
    key_pos = key_start + jnp.arange(key_block, dtype=jnp.int32)
    allowed = (key_pos[None, :] <= query_pos[:, None]) & (seg_keys[None, :] == seg_query[:, None])
    scores = (
        jnp.einsum("tgjd,sgd->gjts", q_block, key_rows, preferred_element_type=jnp.float32)
        * score_scale
    )
    return (scores, allowed, key_start, key_rows)


def attend(q_block, keys, values, seg_all, first_row, key_block, score_scale):
    low_key, high_key = key_bounds(seg_all, first_row, q_block.shape[0], key_block)
    stat_shape = (q_block.shape[1], q_block.shape[2], q_block.shape[0])

    def first_pass(key_index, carry):
        row_max, row_total = carry
        scores, allowed, key_start, key_rows = block_scores(
            q_block, keys, seg_all, first_row, key_index, key_block, score_scale
        )
        new_max = jnp.maximum(row_max, jnp.max(jnp.where(allowed, scores, -1e30), axis=-1))
        row_total = row_total * jnp.exp(row_max - new_max) + jnp.sum(
            jnp.where(allowed, jnp.exp(scores - new_max[..., None]), 0.0), axis=-1
        )
        return (new_max, row_total)

    row_max, row_total = lax.fori_loop(
        low_key,
        high_key,
        first_pass,
        (jnp.full(stat_shape, -1e30, jnp.float32), jnp.zeros(stat_shape, jnp.float32)),
    )
    log_total = row_max + jnp.log(row_total)

    def second_pass(key_index, summed):
        scores, allowed, key_start, key_rows = block_scores(
            q_block, keys, seg_all, first_row, key_index, key_block, score_scale
        )
        probability = jnp.where(allowed, jnp.exp(scores - log_total[..., None]), 0.0).astype(
            jnp.bfloat16
        )
        value_rows = lax.dynamic_slice_in_dim(values, key_start, key_block, 0)
        return summed + jnp.einsum(
            "gjts,sgd->tgjd", probability, value_rows, preferred_element_type=jnp.float32
        )

    summed = lax.fori_loop(low_key, high_key, second_pass, jnp.zeros(q_block.shape, jnp.float32))
    return (summed.astype(jnp.bfloat16), log_total)


def attend_back(
    q_block,
    d_block,
    out_block,
    log_total,
    keys,
    values,
    seg_all,
    first_row,
    key_block,
    score_scale,
    key_grads,
):
    low_key, high_key = key_bounds(seg_all, first_row, q_block.shape[0], key_block)
    d_term = jnp.transpose(
        jnp.sum(d_block.astype(jnp.float32) * out_block.astype(jnp.float32), axis=-1), (1, 2, 0)
    )

    def one_step(key_index, carry):
        q_grad, key_grad, value_grad = carry
        scores, allowed, key_start, key_rows = block_scores(
            q_block, keys, seg_all, first_row, key_index, key_block, score_scale
        )
        probability = jnp.where(allowed, jnp.exp(scores - log_total[..., None]), 0.0)
        value_rows = lax.dynamic_slice_in_dim(values, key_start, key_block, 0)
        d_prob = jnp.einsum(
            "tgjd,sgd->gjts", d_block, value_rows, preferred_element_type=jnp.float32
        )
        d_score = (probability * (d_prob - d_term[..., None])).astype(jnp.bfloat16)
        q_grad = (
            q_grad
            + jnp.einsum("gjts,sgd->tgjd", d_score, key_rows, preferred_element_type=jnp.float32)
            * score_scale
        )
        key_part = (
            jnp.einsum("gjts,tgjd->sgd", d_score, q_block, preferred_element_type=jnp.float32)
            * score_scale
        )
        value_part = jnp.einsum(
            "gjts,tgjd->sgd",
            probability.astype(jnp.bfloat16),
            d_block,
            preferred_element_type=jnp.float32,
        )
        key_grad = lax.dynamic_update_slice_in_dim(
            key_grad,
            lax.dynamic_slice_in_dim(key_grad, key_start, key_block, 0) + key_part,
            key_start,
            0,
        )
        value_grad = lax.dynamic_update_slice_in_dim(
            value_grad,
            lax.dynamic_slice_in_dim(value_grad, key_start, key_block, 0) + value_part,
            key_start,
            0,
        )
        return (q_grad, key_grad, value_grad)

    return lax.fori_loop(
        low_key,
        high_key,
        one_step,
        (jnp.zeros(q_block.shape, jnp.float32), key_grads[0], key_grads[1]),
    )


def forward_product(operand_rows, matrix):
    return (jnp.dot(operand_rows, matrix, preferred_element_type=jnp.float32), operand_rows)


def backward_product(grad_rows, matrix, kept_rows):
    d_rows = jnp.dot(grad_rows, matrix.T, preferred_element_type=jnp.float32)
    d_matrix = jnp.dot(kept_rows.T, grad_rows, preferred_element_type=jnp.float32)
    return (d_rows, d_matrix)


def local(
    x_in,
    seg_ids,
    d_out,
    gain_in,
    w_mix_in,
    conv_w,
    conv_b,
    dt_bias,
    a_log,
    d_skip,
    gain_gate,
    w_mix_out,
    gain_ff,
    w_gate_up,
    w_down,
):
    ctx_count = lax.axis_size("ctx")
    ctx_place = lax.axis_index("ctx")
    at_end = ctx_place == ctx_count - 1
    tokens = x_in[0]
    row_count = tokens.shape[0]
    block_len = row_count // 2
    stream_len = 2 * ctx_count * block_len
    seg_all = seg_ids[0]
    inner_width = gain_gate.shape[0]
    conv_width = conv_w.shape[1]
    mamba_heads = dt_bias.shape[0]
    conv_lag = conv_w.shape[0] - 1
    groups = QHEADS // KVHEADS
    score_scale = HEAD_DIM ** (-0.5)
    key_block = min(KEY_BLOCK, stream_len)
    starts = (ctx_place * block_len, (2 * ctx_count - 1 - ctx_place) * block_len)
    offsets = jnp.arange(block_len, dtype=jnp.int32)
    positions = jnp.concatenate([starts[0] + offsets, starts[1] + offsets])
    matrices = (
        lax.all_gather(w_mix_in, "wa", axis=1, tiled=True),
        lax.all_gather(w_mix_out, "wa", axis=1, tiled=True),
        lax.all_gather(w_gate_up, "wa", axis=1, tiled=True),
        lax.all_gather(w_down, "wa", axis=1, tiled=True),
    )
    m_mix_in, m_mix_out, m_gate_up, m_down = matrices
    x_rows = tokens.astype(jnp.float32)
    h_rows, norm_in_back = jax.vjp(norm_rows, x_rows, gain_in)
    h_bf = h_rows.astype(jnp.bfloat16)
    proj_rows, kept_in = forward_product(h_bf, m_mix_in)
    proj = lax.optimization_barrier(proj_rows.astype(jnp.bfloat16))
    col_q = inner_width + conv_width + mamba_heads
    col_k = col_q + QHEADS * HEAD_DIM
    col_v = col_k + KVHEADS * HEAD_DIM
    gate_part = proj[:, :inner_width].astype(jnp.float32)
    xbc_part = proj[:, inner_width : inner_width + conv_width]
    dt_part = proj[:, inner_width + conv_width : col_q].astype(jnp.float32)
    q_rot = rotate(
        proj[:, col_q:col_k].astype(jnp.float32).reshape(row_count, QHEADS, HEAD_DIM),
        positions,
        1.0,
    ).astype(jnp.bfloat16)
    q_rot = q_rot.reshape(row_count, KVHEADS, groups, HEAD_DIM)
    k_rot = rotate(
        proj[:, col_k:col_v].astype(jnp.float32).reshape(row_count, KVHEADS, HEAD_DIM),
        positions,
        1.0,
    ).astype(jnp.bfloat16)
    k_rot = k_rot.reshape(row_count, KVHEADS * HEAD_DIM)
    v_part = proj[:, col_v:]
    keys_stored, values_stored = (
        lax.all_gather(k_rot, "ctx", axis=0, tiled=True),
        lax.all_gather(v_part, "ctx", axis=0, tiled=True),
    )
    keys = to_natural(keys_stored, ctx_count).reshape(stream_len, KVHEADS, HEAD_DIM)
    values = to_natural(values_stored, ctx_count).reshape(stream_len, KVHEADS, HEAD_DIM)
    att_parts = []
    log_parts = []
    for part_index in range(2):
        q_block = q_rot[part_index * block_len : (part_index + 1) * block_len]
        att_block, log_block = attend(
            q_block, keys, values, seg_all, starts[part_index], key_block, score_scale
        )
        att_parts.append(att_block)
        log_parts.append(log_block)
    attended = jnp.concatenate(att_parts, axis=0)
    tails = (xbc_part[block_len - conv_lag : block_len], xbc_part[row_count - conv_lag :])
    rim = extended_2(jnp.stack([tails[1], tails[0]]), (("ctx", 0),), 1)
    previous = (rim[0], jnp.where(at_end, tails[0], rim[3]))
    seg_exts = []
    seg_befores = []
    extendeds = []
    decays = []
    states = []
    state_backs = []
    for part_index in range(2):
        low_row = part_index * block_len
        index_ext = (
            starts[part_index] - conv_lag + jnp.arange(block_len + conv_lag, dtype=jnp.int32)
        )
        seg_ext = jnp.where(index_ext >= 0, jnp.take(seg_all, jnp.maximum(index_ext, 0)), -1)
        seg_before = jnp.take(seg_all, jnp.maximum(starts[part_index] - 1, 0))
        extended = jnp.concatenate(
            [previous[part_index], xbc_part[low_row : low_row + block_len]], axis=0
        ).astype(jnp.float32)
        (decay_all, end_state), state_back = jax.vjp(
            partial(state_piece, seg_ext, seg_before, inner_width),
            extended,
            dt_part[low_row : low_row + block_len],
            conv_w,
            conv_b,
            dt_bias,
            a_log,
        )
        seg_exts.append(seg_ext)
        seg_befores.append(seg_before)
        extendeds.append(extended)
        decays.append(decay_all)
        states.append(end_state)
        state_backs.append(state_back)
    incoming = state_chain((decays[0], states[0]), (decays[1], states[1]))
    mamba_parts = []
    out_backs = []
    for part_index in range(2):
        low_row = part_index * block_len
        mamba_block, out_back = jax.vjp(
            partial(out_piece, seg_exts[part_index], seg_befores[part_index], inner_width),
            extendeds[part_index],
            dt_part[low_row : low_row + block_len],
            gate_part[low_row : low_row + block_len],
            conv_w,
            conv_b,
            dt_bias,
            a_log,
            d_skip,
            gain_gate,
            incoming[part_index],
        )
        mamba_parts.append(mamba_block)
        out_backs.append(out_back)
    mamba_out = jnp.concatenate(mamba_parts, axis=0).astype(jnp.bfloat16)
    joined = jnp.concatenate([mamba_out, attended.reshape(row_count, QHEADS * HEAD_DIM)], axis=1)
    mix_rows, kept_out = forward_product(joined, m_mix_out)
    x_mid = x_rows + mix_rows
    h2_rows, norm_ff_back = jax.vjp(norm_rows, x_mid, gain_ff)
    h2_bf = h2_rows.astype(jnp.bfloat16)
    gate_up, kept_gate_up = forward_product(h2_bf, m_gate_up)
    act_rows, act_back = jax.vjp(swiglu, gate_up)
    act_bf = act_rows.astype(jnp.bfloat16)
    down_rows, kept_down = forward_product(act_bf, m_down)
    out_rows = (x_mid + down_rows).astype(jnp.bfloat16)
    dy_bf = d_out[0]
    d_act, g_down = backward_product(dy_bf, m_down, kept_down)
    d_gate_up = act_back(d_act)[0].astype(jnp.bfloat16)
    d_h2, g_gate_up = backward_product(d_gate_up, m_gate_up, kept_gate_up)
    d_mid, g_gain_ff = norm_ff_back(d_h2)
    d_mid = d_mid + dy_bf.astype(jnp.float32)
    d_mix = d_mid.astype(jnp.bfloat16)
    d_joined, g_mix_out = backward_product(d_mix, m_mix_out, kept_out)
    d_att = (
        d_joined[:, inner_width:].astype(jnp.bfloat16).reshape(row_count, KVHEADS, groups, HEAD_DIM)
    )
    key_grads = (
        jnp.zeros((stream_len, KVHEADS, HEAD_DIM), jnp.float32),
        jnp.zeros((stream_len, KVHEADS, HEAD_DIM), jnp.float32),
    )
    q_parts = []
    for part_index in range(2):
        low_row = part_index * block_len
        q_grad, key_grad, value_grad = attend_back(
            q_rot[low_row : low_row + block_len],
            d_att[low_row : low_row + block_len],
            att_parts[part_index],
            log_parts[part_index],
            keys,
            values,
            seg_all,
            starts[part_index],
            key_block,
            score_scale,
            key_grads,
        )
        key_grads = (key_grad, value_grad)
        q_parts.append(q_grad)
    own_key_grad, own_value_grad = (
        lax.psum_scatter(
            to_stored(key_grads[0].reshape(stream_len, KVHEADS * HEAD_DIM), ctx_count).astype(
                jnp.bfloat16
            ),
            "ctx",
            scatter_dimension=0,
            tiled=True,
        ).astype(jnp.float32),
        lax.psum_scatter(
            to_stored(key_grads[1].reshape(stream_len, KVHEADS * HEAD_DIM), ctx_count).astype(
                jnp.bfloat16
            ),
            "ctx",
            scatter_dimension=0,
            tiled=True,
        ).astype(jnp.float32),
    )
    d_q = rotate(
        jnp.concatenate(q_parts, axis=0).reshape(row_count, QHEADS, HEAD_DIM), positions, -1.0
    ).reshape(row_count, QHEADS * HEAD_DIM)
    d_k = rotate(own_key_grad.reshape(row_count, KVHEADS, HEAD_DIM), positions, -1.0).reshape(
        row_count, KVHEADS * HEAD_DIM
    )
    direct = []
    for part_index in range(2):
        low_row = part_index * block_len
        direct.append(out_backs[part_index](d_joined[low_row : low_row + block_len, :inner_width]))
    after_second, after_first = state_chain((decays[1], direct[1][9]), (decays[0], direct[0][9]))
    lambdas = (after_first, after_second)
    d_exts = []
    d_dts = []
    small_sums = [
        jnp.zeros_like(conv_w),
        jnp.zeros_like(conv_b),
        jnp.zeros_like(dt_bias),
        jnp.zeros_like(a_log),
        jnp.zeros_like(d_skip),
        jnp.zeros_like(gain_gate),
    ]
    for part_index in range(2):
        d_decay = jnp.sum(lambdas[part_index] * incoming[part_index], axis=(1, 2))
        from_state = state_backs[part_index]((d_decay, lambdas[part_index]))
        from_out = direct[part_index]
        d_exts.append(from_out[0] + from_state[0])
        d_dts.append(from_out[1] + from_state[1])
        small_sums[0] = small_sums[0] + from_out[3] + from_state[2]
        small_sums[1] = small_sums[1] + from_out[4] + from_state[3]
        small_sums[2] = small_sums[2] + from_out[5] + from_state[4]
        small_sums[3] = small_sums[3] + from_out[6] + from_state[5]
        small_sums[4] = small_sums[4] + from_out[7]
        small_sums[5] = small_sums[5] + from_out[8]
    rim_grads = extended_2(
        jnp.stack([d_exts[0][:conv_lag], d_exts[1][:conv_lag]]).astype(jnp.bfloat16),
        (("ctx", 0),),
        1,
    ).astype(jnp.float32)
    extra_first = rim_grads[3] + jnp.where(at_end, d_exts[1][:conv_lag], 0.0)
    extra_second = rim_grads[0]
    d_xbc_first = d_exts[0][conv_lag:] + jnp.pad(extra_first, ((block_len - conv_lag, 0), (0, 0)))
    d_xbc_second = d_exts[1][conv_lag:] + jnp.pad(extra_second, ((block_len - conv_lag, 0), (0, 0)))
    d_gate = jnp.concatenate([direct[0][2], direct[1][2]], axis=0)
    d_proj = jnp.concatenate(
        [
            d_gate,
            jnp.concatenate([d_xbc_first, d_xbc_second], axis=0),
            jnp.concatenate(d_dts, axis=0),
            d_q,
            d_k,
            own_value_grad,
        ],
        axis=1,
    ).astype(jnp.bfloat16)
    d_h, g_mix_in = backward_product(d_proj, m_mix_in, kept_in)
    d_x_norm, g_gain_in = norm_in_back(d_h)
    x_grad = d_mid + d_x_norm
    large = (
        lax.psum_scatter(
            g_mix_in.astype(jnp.bfloat16), "wa", scatter_dimension=1, tiled=True
        ).astype(jnp.float32),
        lax.psum_scatter(
            g_mix_out.astype(jnp.bfloat16), "wa", scatter_dimension=1, tiled=True
        ).astype(jnp.float32),
        lax.psum_scatter(
            g_gate_up.astype(jnp.bfloat16), "wa", scatter_dimension=1, tiled=True
        ).astype(jnp.float32),
        lax.psum_scatter(g_down.astype(jnp.bfloat16), "wa", scatter_dimension=1, tiled=True).astype(
            jnp.float32
        ),
    )
    large = (
        lax.psum_scatter(
            large[0].astype(jnp.bfloat16), "ctx", scatter_dimension=0, tiled=True
        ).astype(jnp.float32),
        lax.psum_scatter(
            large[1].astype(jnp.bfloat16), "ctx", scatter_dimension=0, tiled=True
        ).astype(jnp.float32),
        lax.psum_scatter(
            large[2].astype(jnp.bfloat16), "ctx", scatter_dimension=0, tiled=True
        ).astype(jnp.float32),
        lax.psum_scatter(
            large[3].astype(jnp.bfloat16), "ctx", scatter_dimension=0, tiled=True
        ).astype(jnp.float32),
    )
    small = lax.psum(
        (
            g_gain_in,
            small_sums[0],
            small_sums[1],
            small_sums[2],
            small_sums[3],
            small_sums[4],
            small_sums[5],
            g_gain_ff,
        ),
        ("ctx", "wa"),
    )
    return (
        out_rows[None],
        x_grad[None],
        small[0],
        large[0],
        small[1],
        small[2],
        small[3],
        small[4],
        small[5],
        small[6],
        large[1],
        small[7],
        large[2],
        large[3],
    )


def solution(mesh):
    in_specs = (
        P("wa", "ctx", None),
        P("wa", None),
        P("wa", "ctx", None),
        P(),
        P(None, "wa"),
        P(),
        P(),
        P(),
        P(),
        P(),
        P(),
        P(None, "wa"),
        P(),
        P(None, "wa"),
        P(None, "wa"),
    )
    out_specs = (
        P("wa", "ctx", None),
        P("wa", "ctx", None),
        P(),
        P("ctx", "wa"),
        P(),
        P(),
        P(),
        P(),
        P(),
        P(),
        P("ctx", "wa"),
        P(),
        P("ctx", "wa"),
        P("ctx", "wa"),
    )
    return jax.shard_map(local, mesh=mesh, in_specs=in_specs, out_specs=out_specs, check_vma=False)
```

profile of v0, /device:TPU:0, one launch (start us, length us, event | category | flops | bytes accessed | tf_op | source)
XLA Modules:
  0.0 1250.9 jit_solution(4800721795692995985)
XLA Ops:
  21.8 49.3 %all-gather.32.cloned.1.call-done = bf16[4,1030,1024]{2,1,0:T(8,128)(2,1)} async-done(((bf16[1,1030,1024]{2,1,0:T(8,128)(2,1)}), bf16[4,1030,1024]{2,1,0:T(8,128)(2,1)}) %all-gather.32.cloned.1.call-update) | async-done | bytes 8437776 | tf_op jit(solution)/shard_map/all_gather | solution.py:394
  71.0 8.8 reshape.927
  79.9 6.3 convolution_convert_fusion.2
  103.0 19.0 %all-gather.7 = f32[8,1,24]{2,1,0:T(1,128)S(1)} all-gather(f32[1,1,24]{2,1,0:T(1,128)S(1)} %get-tuple-element.2384), channel_id=1, replica_groups=mesh['ctx'=8,'wa'=4] {'ctx'}, dimensions={0}, use_global_device_ids=true | all-gather | bytes 864 | tf_op jit(solution)/shard_map/all_gather | solution.py:21
  122.3 78.4 %all-gather.24.cloned.1.call-done = f32[192,64,128]{2,1,0:T(8,128)} async-done(((f32[24,64,128]{2,1,0:T(8,128)}), f32[192,64,128]{2,1,0:T(8,128)}) %all-gather.24.cloned.1.call-update) | async-done | bytes 6291472 | tf_op jit(solution)/shard_map/all_gather | solution.py:21
  200.7 10.8 while.158
  231.6 31.7 %all_gather.70 = bf16[1024,128]{1,0:T(8,128)(2,1)S(1)} all-gather(bf16[128,128]{1,0:T(8,128)(2,1)S(1)} %get-tuple-element.2305), channel_id=1, replica_groups=mesh['ctx'=8,'wa'=4] {'ctx'}, dimensions={0}, use_global_device_ids=true | all-gather | bytes 294912 | tf_op jit(solution)/shard_map/all_gather | solution.py:426
  267.6 28.3 %all_gather.71 = bf16[1024,128]{0,1:T(8,128)(2,1)S(1)} all-gather(bf16[128,128]{0,1:T(8,128)(2,1)S(1)} %bitcast.686), channel_id=1, replica_groups=mesh['ctx'=8,'wa'=4] {'ctx'}, dimensions={0}, use_global_device_ids=true | all-gather | bytes 294912 | tf_op jit(solution)/shard_map/all_gather | solution.py:425
  330.3 21.2 %all-reduce.50 = f32[192]{0:T(256)S(1)} all-reduce(f32[192]{0:T(256)} %copy-done.174), channel_id=3, replica_groups=mesh['ctx'=8,'wa'=4] {'ctx'}, use_global_device_ids=true, to_apply=%add.50 | all-reduce | flops 192 | bytes 1536
  352.2 20.7 %while.159 = (s32[]{:T(128)}, f32[24,64,128]{2,1,0:T(8,128)S(1)}, s32[]{:T(128)}, f32[8,24]{1,0:T(8,128)}, f32[8,24,64,128]{3,2,1,0:T(8,128)}, /*index=5*/s32[]{:T(128)}, s32[]{:T(128)}, s32[]{:T(128)}, s32[]{:T(128)}) while((s32[]{:T(128)}, f32[24,64,128]{2,1,0:T(8,128)S(1)}, s32[]{:T(128)}, f32[8,24]{1,0:T(8,128)}, ...), condition=%wide.region_7.10_spmd.clone, body=%wide.region_6.9_spmd.clone.sunk | while | flops 786440 | bytes 2359759 | solution.py:34
  387.6 26.0 %all-gather.20.cloned.1.call-done = bf16[1024,4096]{1,0:T(8,128)(2,1)} async-done(((bf16[1024,1024]{1,0:T(8,128)(2,1)}), bf16[1024,4096]{1,0:T(8,128)(2,1)}) %all-gather.20.cloned.1.call-update) | async-done | bytes 8388624 | tf_op jit(solution)/shard_map/all_gather | solution.py:396
  413.6 6.1 fusion.276
  419.7 30.4 %all-gather.22.cloned.1.call-done = bf16[2048,1024]{1,0:T(8,128)(2,1)} async-done(((bf16[2048,256]{1,0:T(8,128)(2,1)}), bf16[2048,1024]{1,0:T(8,128)(2,1)}) %all-gather.22.cloned.1.call-update) | async-done | bytes 4194320 | tf_op jit(solution)/shard_map/all_gather | solution.py:397
  496.2 7.5 convolution_convert_fusion.1
  504.3 26.0 %all-gather.8 = f32[8,1,24]{2,1,0:T(1,128)S(1)} all-gather(f32[1,1,24]{2,1,0:T(1,128)S(1)} %copy-done.171), channel_id=1, replica_groups=mesh['ctx'=8,'wa'=4] {'ctx'}, dimensions={0}, use_global_device_ids=true | all-gather | bytes 864 | tf_op jit(solution)/shard_map/all_gather | solution.py:21
  532.8 38.6 %all-gather.28.cloned.1.call-done = f32[192,64,128]{2,1,0:T(8,128)} async-done(((f32[24,64,128]{2,1,0:T(8,128)}), f32[192,64,128]{2,1,0:T(8,128)}) %all-gather.28.cloned.1.call-update) | async-done | bytes 6291472 | tf_op jit(solution)/shard_map/all_gather | solution.py:21
  571.4 11.3 while.160
  609.0 7.7 reduce-scatter.18.cloned.1.call-done
  636.6 27.3 %reduce-scatter.26.cloned.1.call-done = bf16[2048,256]{1,0:T(8,128)(2,1)} async-done(((bf16[2048,1024]{1,0:T(8,128)(2,1)}), bf16[2048,256]{1,0:T(8,128)(2,1)}) %reduce-scatter.26.cloned.1.call-update) | async-done | bytes 1048592 | tf_op jit(solution)/shard_map/reduce_scatter | solution.py:624
  683.8 45.1 %reduce-scatter.16.cloned.1.call-done = bf16[128,128]{1,0:T(8,128)(2,1)} async-done(((bf16[1024,128]{1,0:T(8,128)(2,1)}), bf16[128,128]{1,0:T(8,128)(2,1)}) %reduce-scatter.16.cloned.1.call-update) | async-done | bytes 32784 | tf_op jit(solution)/shard_map/reduce_scatter | solution.py:539
  735.2 20.3 %all-reduce.51 = f32[192]{0:T(256)} all-reduce(f32[192]{0:T(256)} %fusion.259), channel_id=6, replica_groups=mesh['ctx'=8,'wa'=4] {'ctx'}, use_global_device_ids=true, to_apply=%add.51 | all-reduce | flops 192 | bytes 1536
  770.1 32.2 %reduce-scatter.22.cloned.1.call-done = bf16[1024,1024]{1,0:T(8,128)(2,1)} async-done(((bf16[1024,4096]{1,0:T(8,128)(2,1)}), bf16[1024,1024]{1,0:T(8,128)(2,1)}) %reduce-scatter.22.cloned.1.call-update) | async-done | bytes 2097168 | tf_op jit(solution)/shard_map/reduce_scatter | solution.py:621
  802.4 101.2 %all-gather.30.cloned.1.call-done = f32[192,64,128]{2,1,0:T(8,128)} async-done(((f32[24,64,128]{2,1,0:T(8,128)}), f32[192,64,128]{2,1,0:T(8,128)}) %all-gather.30.cloned.1.call-update) | async-done | bytes 6291472 | tf_op jit(solution)/shard_map/all_gather | solution.py:21
  903.6 16.1 %while.161 = (s32[]{:T(128)}, f32[24,64,128]{2,1,0:T(8,128)S(1)}, s32[]{:T(128)}, f32[8,24]{1,0:T(8,128)}, f32[8,24,64,128]{3,2,1,0:T(8,128)}, /*index=5*/s32[]{:T(128)}, s32[]{:T(128)}, s32[]{:T(128)}, s32[]{:T(128)}) while((s32[]{:T(128)}, f32[24,64,128]{2,1,0:T(8,128)S(1)}, s32[]{:T(128)}, f32[8,24]{1,0:T(8,128)}, ...), condition=%wide.region_31.34_spmd.clone, body=%wide.region_30.33_spmd.clone.sunk | while | flops 786440 | bytes 2359759 | solution.py:34
  951.4 15.4 %reduce-scatter.30.cloned.1.call-done = bf16[128,128]{1,0:T(8,128)(2,1)} async-done(((bf16[1024,128]{1,0:T(8,128)(2,1)}), bf16[128,128]{1,0:T(8,128)(2,1)}) %reduce-scatter.30.cloned.1.call-update) | async-done | bytes 32784 | tf_op jit(solution)/shard_map/reduce_scatter | solution.py:547
  969.0 5.7 convolution_convert_fusion
  974.7 76.0 %fusion = bf16[1024,1032]{0,1:T(8,128)(2,1)} fusion(bf16[1024,4120]{0,1:T(8,128)(2,1)} %convolution_convert_fusion), kind=kCustom, calls=%all-reduce-scatter | all-reduce-scatter fusion | flops 4227073 | bytes 10551808
  1054.0 11.6 concatenate.104
  1079.3 19.3 %reduce-scatter.28.cloned.1.call-done = bf16[256,256]{1,0:T(8,128)(2,1)} async-done(((bf16[2048,256]{1,0:T(8,128)(2,1)}), bf16[256,256]{1,0:T(8,128)(2,1)}) %reduce-scatter.28.cloned.1.call-update) | async-done | bytes 131088 | tf_op jit(solution)/shard_map/reduce_scatter | solution.py:638
  1100.5 68.9 %reduce-scatter.24.cloned.1.call-done = bf16[128,1024]{1,0:T(8,128)(2,1)} async-done(((bf16[1024,1024]{1,0:T(8,128)(2,1)}), bf16[128,1024]{1,0:T(8,128)(2,1)}) %reduce-scatter.24.cloned.1.call-update) | async-done | bytes 262160 | tf_op jit(solution)/shard_map/reduce_scatter | solution.py:635
  1176.9 41.5 %all-reduce.54 = (f32[1024]{0:T(1024)}, f32[4,1792]{1,0:T(4,128)}, f32[1792]{0:T(1024)}, f32[24]{0:T(128)}, f32[24]{0:T(128)}, /*index=5*/f32[24]{0:T(128)}, f32[1536]{0:T(1024)}, f32[1024]{0:T(1024)}) all-reduce(f32[1024]{0:T(1024)S(1)} %get-tuple-element.2041, ...), channel_id=1, replica_groups=mesh['ctx'=8,'wa'=4] {'ctx','wa'}, use_global_device_ids=true, to_apply=%region_61.64 | all-reduce | flops 12616 | bytes 100928 | tf_op jit(solution)/shard_map/psum | solution.py:642
  1219.4 22.5 %reduce-scatter.32.cloned.1.call-done = bf16[128,1030]{1,0:T(8,128)(2,1)} async-done(((bf16[1024,1030]{1,0:T(8,128)(2,1)}), bf16[128,1030]{1,0:T(8,128)(2,1)}) %reduce-scatter.32.cloned.1.call-update) | async-done | bytes 263696
  (795 shorter events, 366.0 us)
Async XLA Ops:
  7.2 63.8 %all-gather.32.cloned.1.call-start = ((), (), s32[]{:S(2)}) async-start(), calls=%async_computation.23 | async-start | bytes 10567680 | tf_op jit(solution)/shard_map/all_gather | solution.py:394
  7.9 192.8 %all-gather.24.cloned.1.call-start = ((), (), s32[]{:S(2)}) async-start(), calls=%async_computation.19 | async-start | bytes 7077888 | tf_op jit(solution)/shard_map/all_gather | solution.py:21
  86.4 5.6 collective-permute-start.1
  88.5 227.9 %copy-start.57 = (f32[64,24]{1,0:T(8,128)}, f32[64,24]{1,0:T(8,128)S(1)}, u32[]{:S(2)}) copy-start(f32[64,24]{1,0:T(8,128)S(1)} %reduce_window_sum.48) | copy-start | bytes 18436
  88.6 228.6 %copy-start.59 = (f32[64,24]{1,0:T(8,128)}, f32[64,24]{1,0:T(8,128)S(1)}, u32[]{:S(2)}) copy-start(f32[64,24]{1,0:T(8,128)S(1)} %reduce_window_sum.49) | copy-start | bytes 18436
  92.0 5.7 collective-permute-start
  101.6 250.6 %all-gather.26.cloned.1.call-start = ((), (), s32[]{:S(2)}) async-start(), calls=%async_computation.20 | async-start | bytes 7077888 | tf_op jit(solution)/shard_map/all_gather | solution.py:21
  103.0 108.7 %copy-start.75 = (f32[64,24]{0,1:T(8,128)}, f32[64,24]{0,1:T(8,128)S(1)}, u32[]{:S(2)}) copy-start(f32[64,24]{0,1:T(8,128)S(1)} %copy.669) | copy-start | bytes 18436
  214.8 169.4 %all-gather.18.cloned.1.call-start = ((), (), s32[]{:S(2)}) async-start(), calls=%async_computation.9 | async-start | bytes 5242880 | tf_op jit(solution)/shard_map/all_gather | solution.py:395
  215.4 198.2 %all-gather.20.cloned.1.call-start = ((), (), s32[]{:S(2)}) async-start(), calls=%async_computation.10 | async-start | bytes 10485760 | tf_op jit(solution)/shard_map/all_gather | solution.py:396
  216.0 234.1 %all-gather.22.cloned.1.call-start = ((), (), s32[]{:S(2)}) async-start(), calls=%async_computation.11 | async-start | bytes 5242880 | tf_op jit(solution)/shard_map/all_gather | solution.py:397
  216.5 354.8 %all-gather.28.cloned.1.call-start = ((), (), s32[]{:S(2)}) async-start(), calls=%async_computation.21 | async-start | bytes 7077888 | tf_op jit(solution)/shard_map/all_gather | solution.py:21
  472.2 144.5 %reduce-scatter.18.cloned.1.call-start = ((), (), s32[]{:S(2)}) async-start(), calls=%async_computation.13 | async-start | bytes 5242880 | tf_op jit(solution)/shard_map/reduce_scatter | solution.py:618
  476.5 187.4 %reduce-scatter.26.cloned.1.call-start = ((), (), s32[]{:S(2)}) async-start(), calls=%async_computation.17 | async-start | bytes 5242880 | tf_op jit(solution)/shard_map/reduce_scatter | solution.py:624
  481.7 247.2 %reduce-scatter.16.cloned.1.call-start = ((), (), s32[]{:S(2)}) async-start(), calls=%async_computation.12 | async-start | bytes 294912 | tf_op jit(solution)/shard_map/reduce_scatter | solution.py:539
  496.2 306.1 %reduce-scatter.22.cloned.1.call-start = ((), (), s32[]{:S(2)}) async-start(), calls=%async_computation.15 | async-start | bytes 10485760 | tf_op jit(solution)/shard_map/reduce_scatter | solution.py:621
  503.7 399.9 %all-gather.30.cloned.1.call-start = ((), (), s32[]{:S(2)}) async-start(), calls=%async_computation.22 | async-start | bytes 7077888 | tf_op jit(solution)/shard_map/all_gather | solution.py:21
  585.6 381.1 %reduce-scatter.30.cloned.1.call-start = ((), (), s32[]{:S(2)}) async-start(), calls=%async_computation.24 | async-start | bytes 294912 | tf_op jit(solution)/shard_map/reduce_scatter | solution.py:547
  599.9 477.8 %reduce-scatter.20.cloned.1.call-start = ((), (), s32[]{:S(2)}) async-start(), calls=%async_computation.14 | async-start | bytes 1179648 | tf_op jit(solution)/shard_map/reduce_scatter | solution.py:632
  616.7 482.0 %reduce-scatter.28.cloned.1.call-start = ((), (), s32[]{:S(2)}) async-start(), calls=%async_computation.18 | async-start | bytes 1179648 | tf_op jit(solution)/shard_map/reduce_scatter | solution.py:638
  663.9 505.4 %reduce-scatter.24.cloned.1.call-start = ((), (), s32[]{:S(2)}) async-start(), calls=%async_computation.16 | async-start | bytes 2359296 | tf_op jit(solution)/shard_map/reduce_scatter | solution.py:635
  802.3 439.6 %reduce-scatter.32.cloned.1.call-start = ((), (), s32[]{:S(2)}) async-start(), calls=%async_computation.25 | async-start | bytes 2654208
  930.4 17.9 %collective-permute-start.3 = (bf16[1,3,1792]{2,1,0:T(4,128)(2,1)S(1)}, bf16[1,3,1792]{2,1,0:T(4,128)(2,1)}, u32[]{:S(2)}, u32[]{:S(2)}) collective-permute-start(bf16[1,3,1792]{2,1,0:T(4,128)(2,1)S(1)} %fusion.257), channel_id=1, source_target_pairs={{4,0},{8,4},{12,8},{16,12},{20,16},{24,20},{28,24},{5,1},{9,5},{13... | collective-permute-start | bytes 32264 | tf_op jit(solution)/shard_map/ppermute | solution.py:47
  932.3 15.9 %collective-permute-start.2 = (bf16[1,3,1792]{2,1,0:T(4,128)(2,1)S(1)}, bf16[1,3,1792]{2,1,0:T(4,128)(2,1)}, u32[]{:S(2)}, u32[]{:S(2)}) collective-permute-start(bf16[1,3,1792]{2,1,0:T(4,128)(2,1)S(1)} %get-tuple-element.2275), channel_id=1, source_target_pairs={{0,4},{4,8},{8,12},{12,16},{16,20},{20,24},{24,28},{1,5},{5,9},{9,... | collective-permute-start | bytes 32264 | tf_op jit(solution)/shard_map/ppermute | solution.py:45
  1051.5 2.5 collective-permute-start.4
  1073.5 97.8 %copy-start.126 = (f32[1792]{0:T(1024)S(1)}, f32[1792]{0:T(1024)}, u32[]{:S(2)}) copy-start(f32[1792]{0:T(1024)} %get-tuple-element.2049) | copy-start | bytes 21508
  1073.5 97.8 %copy-start.125 = (f32[1792]{0:T(1024)S(1)}, f32[1792]{0:T(1024)}, u32[]{:S(2)}) copy-start(f32[1792]{0:T(1024)} %get-tuple-element.2050) | copy-start | bytes 21508
  1073.5 97.8 %copy-start.170 = (f32[24]{0:T(128)S(1)}, f32[24]{0:T(128)}, u32[]{:S(2)}) copy-start(f32[24]{0:T(128)} %get-tuple-element.2257) | copy-start | bytes 292
  1073.5 97.8 %copy-start.178 = (f32[24]{0:T(128)S(1)}, f32[24]{0:T(128)}, u32[]{:S(2)}) copy-start(f32[24]{0:T(128)} %param.46) | copy-start | bytes 292
  1073.5 97.9 %copy-start.110 = (f32[1792]{0:T(1024)S(1)}, f32[1792]{0:T(1024)}, u32[]{:S(2)}) copy-start(f32[1792]{0:T(1024)} %get-tuple-element.2052) | copy-start | bytes 21508
  1073.6 97.9 %copy-start.111 = (f32[1792]{0:T(1024)S(1)}, f32[1792]{0:T(1024)}, u32[]{:S(2)}) copy-start(f32[1792]{0:T(1024)} %get-tuple-element.2054) | copy-start | bytes 21508
  1073.6 97.9 %copy-start.112 = (f32[1792]{0:T(1024)S(1)}, f32[1792]{0:T(1024)}, u32[]{:S(2)}) copy-start(f32[1792]{0:T(1024)} %get-tuple-element.2053) | copy-start | bytes 21508
  (174 other events, 3963.7 us)
Sparse Core Ops, SparseCore 0:
  9.6 61.4 all-gather.31
  101.7 98.9 all-gather.23
  214.9 104.0 all-gather.25
  320.5 33.3 all-gather.17
  355.2 58.2 all-gather.19
  415.0 35.0 all-gather.21
  472.3 99.0 all-gather.27
  573.9 42.7 reduce-scatter.17
  619.3 44.5 reduce-scatter.25
  667.6 61.2 reduce-scatter.15
  731.5 70.7 reduce-scatter.21
  804.6 98.9 all-gather.29
  907.3 59.4 reduce-scatter.29
  970.4 62.4 reduce-scatter.19
  1036.2 62.4 reduce-scatter.27
  1102.5 66.8 reduce-scatter.23
  1173.1 68.7 reduce-scatter.31
where the time goes:
time: 1270 us; the launch traced here: 1250 us
  waiting for transfers between devices  569 us (45%)
  blocking collectives  264 us (21%)
  matrix products  128 us (10%)
  other arithmetic  126 us (10%)
  local copies, waits for them, and re-layouts  121 us (10%)
  between operations  27.7 us (2%)
  starting transfers between devices  14.3 us (1%)
    all_gather x4, waiting for transfers between devices, prefix(): everything = jax.tree.map(lambda part: lax.all_gather(part, axis), shard)  218 us
    unnamed x3, blocking collectives  118 us
    reduce_scatter x1, waiting for transfers between devices, local(): lax.psum_scatter(large[2].astype(jnp.bfloat16), 'ctx', scatter_dimension=...  68.9 us
    all_gather x1, waiting for transfers between devices, local(): lax.all_gather(w_mix_in, 'wa', axis=1, tiled=True)  49.3 us
    reduce_scatter x1, waiting for transfers between devices, local(): lax.psum_scatter(to_stored(key_grads[0].reshape(stream_len, KVHEADS * HEA...  45.1 us
    all_gather x2, blocking collectives, prefix(): everything = jax.tree.map(lambda part: lax.all_gather(part, axis), shard)  45 us
    select_n x48, other arithmetic, lap(): return jax.tree.map(lambda a, b: jnp.where(reached, a, b), new, before)  42.8 us
    psum x1, blocking collectives, local(): lax.psum((g_gain_in, small_sums[0], small_sums[1], small_sums[2], small_s...  41.5 us
  transfers between devices with their start and end apart: 22, of which 16 were waited for; matrix products, arithmetic and copies ran while one was open for 31% of the time, Pallas kernels for 0%

commit v1 on v0

v1 whole, which is shorter than its diff:
```python
import jax
import jax.numpy as jnp
from jax import lax
from jax.sharding import PartitionSpec as P

QHEADS = 8
KVHEADS = 2
HEAD_DIM = 64


EPS = 1e-05
ROPE_BASE = 100000000000.0
HIGH = lax.Precision.HIGHEST


def extended_2(cells, sides, width):
    for axis, dim in sides:
        count = lax.axis_size(axis)
        ends = count - 1
        head = lax.slice_in_dim(cells, 0, width, axis=dim)
        tail = lax.slice_in_dim(cells, cells.shape[dim] - width, cells.shape[dim], axis=dim)
        cells = jnp.concatenate(
            [
                lax.ppermute(tail, axis, [(i, (i + 1) % count) for i in range(ends)]),
                cells,
                lax.ppermute(head, axis, [((i + 1) % count, i) for i in range(ends)]),
            ],
            axis=dim,
        )
    return cells


def norm_rows(values, gain):
    return values * lax.rsqrt(jnp.mean(values * values, axis=-1, keepdims=True) + EPS) * gain


def swiglu(mixed):
    half_size = mixed.shape[-1] // 2
    return jax.nn.silu(mixed[:, :half_size]) * mixed[:, half_size:]


def rotate(values, positions, direction):
    head_size = values.shape[-1]
    half_size = head_size // 2
    frequency = ROPE_BASE ** (-2.0 * jnp.arange(half_size, dtype=jnp.float32) / head_size)
    angles = positions.astype(jnp.float32)[:, None] * frequency[None, :]
    cosine = jnp.cos(angles)[:, None, :]
    sine_part = direction * jnp.sin(angles)[:, None, :]
    first_half = values[..., :half_size]
    second_half = values[..., half_size:]
    return jnp.concatenate(
        [
            first_half * cosine - second_half * sine_part,
            second_half * cosine + first_half * sine_part,
        ],
        axis=-1,
    )


def conv_rows(extended, seg_ext, conv_w, conv_b):
    conv_lag = conv_w.shape[0] - 1
    length = extended.shape[0] - conv_lag
    summed = jnp.zeros((length, extended.shape[1]), jnp.float32) + conv_b[None, :]
    for tap_index in range(conv_lag + 1):
        same_doc = (seg_ext[tap_index : tap_index + length] == seg_ext[conv_lag:]).astype(
            jnp.float32
        )
        summed = (
            summed
            + conv_w[tap_index][None, :]
            * extended[tap_index : tap_index + length]
            * same_doc[:, None]
        )
    return jax.nn.silu(summed)


def block_inputs(extended, seg_ext, raw_dt, conv_w, conv_b, dt_bias, a_log, inner_width):
    mixed = conv_rows(extended, seg_ext, conv_w, conv_b)
    length = mixed.shape[0]
    mamba_heads = dt_bias.shape[0]
    state_size = (mixed.shape[1] - inner_width) // 2
    inputs_x = mixed[:, :inner_width].reshape(length, mamba_heads, inner_width // mamba_heads)
    b_rows = mixed[:, inner_width : inner_width + state_size]
    c_rows = mixed[:, inner_width + state_size :]
    step_dt = jax.nn.softplus(raw_dt + dt_bias[None, :])
    log_decay = -step_dt * jnp.exp(a_log)[None, :]
    return (inputs_x, b_rows, c_rows, step_dt, log_decay)


def block_state(inputs_x, b_rows, step_dt, log_decay, seg_block, seg_before):
    cumulative = jnp.cumsum(log_decay, axis=0)
    keep_end = (seg_block == seg_block[-1]).astype(jnp.float32)
    weights = jnp.exp(cumulative[-1][None, :] - cumulative) * keep_end[:, None] * step_dt
    end_state = jnp.einsum("shp,sn->hpn", weights[:, :, None] * inputs_x, b_rows, precision=HIGH)
    decay_all = jnp.exp(cumulative[-1]) * (seg_block[-1] == seg_before).astype(jnp.float32)
    return (decay_all, end_state)


def block_output(
    inputs_x, b_rows, c_rows, step_dt, log_decay, d_skip, seg_block, seg_before, state_in
):
    length = inputs_x.shape[0]
    cumulative = jnp.cumsum(log_decay, axis=0)
    lower_tri = jnp.arange(length)[:, None] >= jnp.arange(length)[None, :]
    allowed = lower_tri & (seg_block[:, None] == seg_block[None, :])
    across = cumulative.T
    exponent = jnp.where(allowed[None], across[:, :, None] - across[:, None, :], -jnp.inf)
    intersection = jnp.dot(c_rows, b_rows.T, precision=HIGH)
    mixing = jnp.exp(exponent) * intersection[None] * step_dt.T[:, None, :]
    inner_out = jnp.einsum("hts,shp->thp", mixing, inputs_x, precision=HIGH)
    carried = (seg_block == seg_before).astype(jnp.float32)
    from_state = (
        jnp.einsum("tn,hpn->thp", c_rows, state_in, precision=HIGH)
        * (jnp.exp(cumulative) * carried[:, None])[:, :, None]
    )
    return inner_out + from_state + d_skip[None, :, None] * inputs_x


def gated_norm(outputs, gate_rows, gain_gate):
    return norm_rows(outputs * jax.nn.silu(gate_rows), gain_gate)


def block_chain(states, decays, reverse):
    order = range(states.shape[0])
    order = order[::-1] if reverse else order
    held = jnp.zeros(states.shape[1:], jnp.float32)
    before = [None] * states.shape[0]
    for at in order:
        before[at] = held.astype(jnp.bfloat16)
        held = decays[at][:, None] * held + states[at].astype(jnp.float32)
    return jnp.stack(before)


def swap_blocks(parts):
    return jnp.concatenate([parts[:, 0], parts[::-1, 1]], axis=0)


def unswap_blocks(blocks, count):
    return jnp.stack([blocks[:count], blocks[count:][::-1]], axis=1)


def cut_rows(states, count):
    rows = states.shape[1] * states.shape[2] // count
    cut = states.astype(jnp.bfloat16).reshape(2, count, rows, states.shape[3])
    return jnp.swapaxes(cut, 0, 1)


def join_rows(cut, shape):
    return jnp.swapaxes(cut, 0, 1).reshape(shape).astype(jnp.float32)


def swap_axis(parts):
    return lax.all_to_all(parts, "ctx", split_axis=0, concat_axis=0, tiled=True)


def states_before(states, decays, ctx_count):
    heads, width, size = states.shape[1:]
    rows = heads * width // ctx_count
    cut = cut_rows(states, ctx_count)
    high = decays.astype(jnp.bfloat16)
    low = (decays - high.astype(jnp.float32)).astype(jnp.bfloat16)
    marks = jnp.pad(jnp.stack([high, low], axis=1), ((0, 0), (0, 14), (0, size - heads)))
    marks = jnp.broadcast_to(marks[None], (ctx_count,) + marks.shape)
    got = swap_axis(jnp.concatenate([cut, marks], axis=2))
    all_decays = (got[:, :, rows, :heads].astype(jnp.float32)) + got[:, :, rows + 1, :heads].astype(
        jnp.float32
    )
    all_decays = jnp.repeat(swap_blocks(all_decays), width, axis=1)
    my_decays = lax.dynamic_slice_in_dim(all_decays, lax.axis_index("ctx") * rows, rows, 1)
    before = block_chain(swap_blocks(got[:, :, :rows]), my_decays, False)
    back = swap_axis(unswap_blocks(before, ctx_count))
    return join_rows(back, states.shape), my_decays


def grads_after(grads, my_decays, ctx_count):
    got = swap_axis(cut_rows(grads, ctx_count))
    after = block_chain(swap_blocks(got), my_decays, True)
    return join_rows(swap_axis(unswap_blocks(after, ctx_count)), grads.shape)


def by_columns(values):
    return lax.all_to_all(values, "wa", split_axis=1, concat_axis=0, tiled=True)


def shares(values, count):
    return values.reshape(values.shape[0], count, values.shape[1] // count)


def by_columns_of(first, second, third, count):
    cuts = [shares(first, count), shares(second, count), shares(third, count)]
    joined = jnp.concatenate(cuts, axis=2)
    got = by_columns(joined.reshape(joined.shape[0], -1))
    one = cuts[0].shape[2]
    two = one + cuts[1].shape[2]
    return (got[:, :one], got[:, one:two], got[:, two:])


def column_grad(kept_rows, grad_cols):
    partial_grad = jnp.einsum("tk,tn->kn", kept_rows, grad_cols, preferred_element_type=jnp.float32)
    return lax.psum_scatter(
        partial_grad.astype(jnp.bfloat16), "ctx", scatter_dimension=0, tiled=True
    ).astype(jnp.float32)


def to_stored(natural, ctx_count):
    tail_shape = natural.shape[1:]
    half_len = natural.shape[0] // 2
    block_len = half_len // ctx_count
    leading = natural[:half_len].reshape((ctx_count, block_len) + tail_shape)
    trailing = natural[half_len:].reshape((ctx_count, block_len) + tail_shape)[::-1]
    return jnp.stack([leading, trailing], axis=1).reshape(natural.shape)


def local(
    x_in,
    seg_ids,
    d_out,
    gain_in,
    w_mix_in,
    conv_w,
    conv_b,
    dt_bias,
    a_log,
    d_skip,
    gain_gate,
    w_mix_out,
    gain_ff,
    w_gate_up,
    w_down,
):
    ctx_count = lax.axis_size("ctx")
    wa_count = lax.axis_size("wa")
    ctx_place = lax.axis_index("ctx")
    at_end = ctx_place == ctx_count - 1
    tokens = x_in[0]
    row_count = tokens.shape[0]
    block_len = row_count // 2
    seg_all = seg_ids[0]
    inner_width = gain_gate.shape[0]
    conv_width = conv_w.shape[1]
    mamba_heads = dt_bias.shape[0]
    conv_lag = conv_w.shape[0] - 1
    groups = QHEADS // KVHEADS
    score_scale = HEAD_DIM ** (-0.5)
    starts = (ctx_place * block_len, (2 * ctx_count - 1 - ctx_place) * block_len)
    offsets = jnp.arange(block_len, dtype=jnp.int32)
    positions = jnp.concatenate([starts[0] + offsets, starts[1] + offsets])
    x_rows = tokens.astype(jnp.float32)
    h_rows, norm_in_back = jax.vjp(norm_rows, x_rows, gain_in)
    h_all = lax.all_gather(h_rows.astype(jnp.bfloat16), "wa", axis=0, tiled=True)
    proj_cols = jnp.dot(h_all, w_mix_in, preferred_element_type=jnp.float32).astype(jnp.bfloat16)
    proj = lax.all_to_all(proj_cols, "wa", split_axis=0, concat_axis=1, tiled=True)
    proj = lax.optimization_barrier(proj)
    m_mix_out = lax.all_gather(w_mix_out, "wa", axis=1, tiled=True)
    m_down = lax.all_gather(w_down, "wa", axis=1, tiled=True)
    m_gate_up = lax.all_gather(w_gate_up, "wa", axis=1, tiled=True)
    col_q = inner_width + conv_width + mamba_heads
    col_k = col_q + QHEADS * HEAD_DIM
    col_v = col_k + KVHEADS * HEAD_DIM
    kv_width = KVHEADS * HEAD_DIM
    gate_part = proj[:, :inner_width].astype(jnp.float32)
    xbc_part = proj[:, inner_width : inner_width + conv_width]
    dt_part = proj[:, inner_width + conv_width : col_q].astype(jnp.float32)
    q_rot = rotate(
        proj[:, col_q:col_k].astype(jnp.float32).reshape(row_count, QHEADS, HEAD_DIM),
        positions,
        1.0,
    ).astype(jnp.bfloat16)
    q_rot = q_rot.reshape(row_count, KVHEADS, groups, HEAD_DIM)
    k_rot = rotate(
        proj[:, col_k:col_v].astype(jnp.float32).reshape(row_count, KVHEADS, HEAD_DIM),
        positions,
        1.0,
    ).astype(jnp.bfloat16)
    kv_all = lax.all_gather(
        jnp.concatenate([k_rot.reshape(row_count, kv_width), proj[:, col_v:]], axis=1),
        "ctx",
        axis=0,
        tiled=True,
    )
    tails = (xbc_part[block_len - conv_lag : block_len], xbc_part[row_count - conv_lag :])
    rim = extended_2(jnp.stack([tails[1], tails[0]]), (("ctx", 0),), 1)
    previous = (rim[0], jnp.where(at_end, tails[0], rim[3]))
    seg_exts = []
    seg_befores = []
    extendeds = []
    for part_index in range(2):
        low_row = part_index * block_len
        index_ext = (
            starts[part_index] - conv_lag + jnp.arange(block_len + conv_lag, dtype=jnp.int32)
        )
        seg_exts.append(jnp.where(index_ext >= 0, jnp.take(seg_all, jnp.maximum(index_ext, 0)), -1))
        seg_befores.append(jnp.take(seg_all, jnp.maximum(starts[part_index] - 1, 0)))
        extendeds.append(
            jnp.concatenate(
                [previous[part_index], xbc_part[low_row : low_row + block_len]], axis=0
            ).astype(jnp.float32)
        )
    seg_ext = jnp.stack(seg_exts)
    seg_before = jnp.stack(seg_befores)
    seg_block = seg_ext[:, conv_lag:]

    def all_inputs(extended, raw_dt, conv_w, conv_b, dt_bias, a_log):
        return jax.vmap(
            lambda ext, seg, raw: block_inputs(
                ext, seg, raw, conv_w, conv_b, dt_bias, a_log, inner_width
            )
        )(extended, seg_ext, raw_dt)

    def all_states(inputs_x, b_rows, step_dt, log_decay):
        return jax.vmap(block_state)(inputs_x, b_rows, step_dt, log_decay, seg_block, seg_before)

    def all_outputs(
        inputs_x, b_rows, c_rows, step_dt, log_decay, gate_rows, d_skip, gain_gate, state_in
    ):
        outputs = jax.vmap(block_output, in_axes=(0, 0, 0, 0, 0, None, 0, 0, 0))(
            inputs_x, b_rows, c_rows, step_dt, log_decay, d_skip, seg_block, seg_before, state_in
        )
        return gated_norm(outputs.reshape(row_count, inner_width), gate_rows, gain_gate)

    (inputs_x, b_rows, c_rows, step_dt, log_decay), inputs_back = jax.vjp(
        all_inputs,
        jnp.stack(extendeds),
        dt_part.reshape(2, block_len, mamba_heads),
        conv_w,
        conv_b,
        dt_bias,
        a_log,
    )
    (decays, states), states_back = jax.vjp(all_states, inputs_x, b_rows, step_dt, log_decay)
    incoming, my_decays = states_before(states, decays, ctx_count)

    keys = kv_all[:, :kv_width].reshape(-1, KVHEADS, HEAD_DIM)
    values = kv_all[:, kv_width:].reshape(-1, KVHEADS, HEAD_DIM)
    key_seg = to_stored(seg_all, ctx_count)
    key_pos = to_stored(jnp.arange(seg_all.shape[0], dtype=jnp.int32), ctx_count)
    query_seg = seg_block.reshape(row_count)
    allowed = (key_pos[None, :] <= positions[:, None]) & (key_seg[None, :] == query_seg[:, None])
    scores = (
        jnp.einsum("tgjd,sgd->gjts", q_rot, keys, preferred_element_type=jnp.float32) * score_scale
    )
    row_max = jnp.max(jnp.where(allowed, scores, -1e30), axis=-1, keepdims=True)
    raised = jnp.where(allowed, jnp.exp(scores - row_max), 0.0)
    probability = raised * (1.0 / jnp.sum(raised, axis=-1, keepdims=True))
    prob_bf = probability.astype(jnp.bfloat16)
    attended = jnp.einsum(
        "gjts,sgd->tgjd", prob_bf, values, preferred_element_type=jnp.float32
    ).astype(jnp.bfloat16)

    mamba_out, out_back = jax.vjp(
        all_outputs,
        inputs_x,
        b_rows,
        c_rows,
        step_dt,
        log_decay,
        gate_part,
        d_skip,
        gain_gate,
        incoming,
    )
    joined = jnp.concatenate(
        [mamba_out.astype(jnp.bfloat16), attended.reshape(row_count, QHEADS * HEAD_DIM)], axis=1
    )
    x_mid = x_rows + jnp.dot(joined, m_mix_out, preferred_element_type=jnp.float32)
    h2_rows, norm_ff_back = jax.vjp(norm_rows, x_mid, gain_ff)
    h2_bf = h2_rows.astype(jnp.bfloat16)
    gate_up = jnp.dot(h2_bf, m_gate_up, preferred_element_type=jnp.float32)
    act_rows, act_back = jax.vjp(swiglu, gate_up)
    act_bf = act_rows.astype(jnp.bfloat16)
    kept_all = lax.all_gather(
        jnp.concatenate([joined, h2_bf, act_bf], axis=1), "wa", axis=0, tiled=True
    )
    out_rows = (x_mid + jnp.dot(act_bf, m_down, preferred_element_type=jnp.float32)).astype(
        jnp.bfloat16
    )
    dy_bf = d_out[0]
    d_act = jnp.dot(dy_bf, m_down.T, preferred_element_type=jnp.float32)
    d_gate_up = act_back(d_act)[0].astype(jnp.bfloat16)
    d_h2 = jnp.dot(d_gate_up, m_gate_up.T, preferred_element_type=jnp.float32)
    d_mid, g_gain_ff = norm_ff_back(d_h2)
    d_mid = d_mid + dy_bf.astype(jnp.float32)
    d_mix = d_mid.astype(jnp.bfloat16)
    d_joined = jnp.dot(d_mix, m_mix_out.T, preferred_element_type=jnp.float32)

    from_out = out_back(d_joined[:, :inner_width])
    lambdas = grads_after(from_out[8], my_decays, ctx_count)

    d_att = (
        d_joined[:, inner_width:].astype(jnp.bfloat16).reshape(row_count, KVHEADS, groups, HEAD_DIM)
    )
    d_term = jnp.transpose(
        jnp.sum(d_att.astype(jnp.float32) * attended.astype(jnp.float32), axis=-1), (1, 2, 0)
    )
    d_prob = jnp.einsum("tgjd,sgd->gjts", d_att, values, preferred_element_type=jnp.float32)
    d_score = (probability * (d_prob - d_term[..., None])).astype(jnp.bfloat16)
    q_grad = (
        jnp.einsum("gjts,sgd->tgjd", d_score, keys, preferred_element_type=jnp.float32)
        * score_scale
    )
    key_grad = (
        jnp.einsum("gjts,tgjd->sgd", d_score, q_rot, preferred_element_type=jnp.float32)
        * score_scale
    )
    value_grad = jnp.einsum("gjts,tgjd->sgd", prob_bf, d_att, preferred_element_type=jnp.float32)
    own_kv_grad = lax.psum_scatter(
        jnp.concatenate(
            [key_grad.reshape(-1, kv_width), value_grad.reshape(-1, kv_width)], axis=1
        ).astype(jnp.bfloat16),
        "ctx",
        scatter_dimension=0,
        tiled=True,
    ).astype(jnp.float32)
    d_q = rotate(q_grad.reshape(row_count, QHEADS, HEAD_DIM), positions, -1.0).reshape(
        row_count, QHEADS * HEAD_DIM
    )
    d_k = rotate(
        own_kv_grad[:, :kv_width].reshape(row_count, KVHEADS, HEAD_DIM), positions, -1.0
    ).reshape(row_count, kv_width)

    grad_cols = by_columns_of(d_mix, d_gate_up, dy_bf, wa_count)
    cat_width = joined.shape[1]
    model_width = tokens.shape[1]
    g_mix_out = column_grad(kept_all[:, :cat_width], grad_cols[0])
    g_gate_up = column_grad(kept_all[:, cat_width : cat_width + model_width], grad_cols[1])
    g_down = column_grad(kept_all[:, cat_width + model_width :], grad_cols[2])

    d_decay = jnp.sum(lambdas * incoming, axis=(2, 3))
    from_state = states_back((d_decay, lambdas))
    from_inputs = inputs_back(
        (
            from_out[0] + from_state[0],
            from_out[1] + from_state[1],
            from_out[2],
            from_out[3] + from_state[2],
            from_out[4] + from_state[3],
        )
    )
    d_exts, d_dts = from_inputs[0], from_inputs[1]
    rim_grads = extended_2(d_exts[:, :conv_lag].astype(jnp.bfloat16), (("ctx", 0),), 1).astype(
        jnp.float32
    )
    extra_first = rim_grads[3] + jnp.where(at_end, d_exts[1][:conv_lag], 0.0)
    extra_second = rim_grads[0]
    d_xbc_first = d_exts[0][conv_lag:] + jnp.pad(extra_first, ((block_len - conv_lag, 0), (0, 0)))
    d_xbc_second = d_exts[1][conv_lag:] + jnp.pad(extra_second, ((block_len - conv_lag, 0), (0, 0)))
    d_proj = jnp.concatenate(
        [
            from_out[5].astype(jnp.bfloat16),
            jnp.concatenate([d_xbc_first, d_xbc_second], axis=0).astype(jnp.bfloat16),
            d_dts.reshape(row_count, mamba_heads).astype(jnp.bfloat16),
            d_q.astype(jnp.bfloat16),
            d_k.astype(jnp.bfloat16),
            own_kv_grad[:, kv_width:].astype(jnp.bfloat16),
        ],
        axis=1,
    )
    d_proj_cols = by_columns(d_proj)
    g_mix_in = column_grad(h_all, d_proj_cols)
    d_h = lax.psum_scatter(
        jnp.dot(d_proj_cols, w_mix_in.T, preferred_element_type=jnp.float32).astype(jnp.bfloat16),
        "wa",
        scatter_dimension=0,
        tiled=True,
    ).astype(jnp.float32)
    d_x_norm, g_gain_in = norm_in_back(d_h)
    x_grad = d_mid + d_x_norm
    small_parts = (
        g_gain_in,
        from_inputs[2],
        from_inputs[3],
        from_inputs[4],
        from_inputs[5],
        from_out[6],
        from_out[7],
        g_gain_ff,
    )
    flat = jnp.concatenate([part.reshape(-1) for part in small_parts])
    flat = jnp.pad(flat, (0, -flat.shape[0] % 1024)).reshape(-1, 128)
    flat = jnp.sum(lax.all_gather(flat, ("ctx", "wa"), axis=0), axis=0).reshape(-1)
    small = []
    place = 0
    for part in small_parts:
        small.append(flat[place : place + part.size].reshape(part.shape))
        place += part.size
    return (
        out_rows[None],
        x_grad[None],
        small[0],
        g_mix_in,
        small[1],
        small[2],
        small[3],
        small[4],
        small[5],
        small[6],
        g_mix_out,
        small[7],
        g_gate_up,
        g_down,
    )


def solution(mesh):
    in_specs = (
        P("wa", "ctx", None),
        P("wa", None),
        P("wa", "ctx", None),
        P(),
        P(None, "wa"),
        P(),
        P(),
        P(),
        P(),
        P(),
        P(),
        P(None, "wa"),
        P(),
        P(None, "wa"),
        P(None, "wa"),
    )
    out_specs = (
        P("wa", "ctx", None),
        P("wa", "ctx", None),
        P(),
        P("ctx", "wa"),
        P(),
        P(),
        P(),
        P(),
        P(),
        P(),
        P("ctx", "wa"),
        P(),
        P("ctx", "wa"),
        P("ctx", "wa"),
    )
    return jax.shard_map(local, mesh=mesh, in_specs=in_specs, out_specs=out_specs, check_vma=False)
```

time: 1270 us -> 850 us (0.67)
  waiting for transfers between devices: 569 us -> 396 us
  blocking collectives: 264 us -> 97.2 us
  other arithmetic: 126 us -> 90.1 us
  matrix products: 128 us -> 97.7 us
  starting transfers between devices: 14.3 us -> 37.6 us
  local copies, waits for them, and re-layouts: 121 us -> 99.9 us
    all_gather x8 -> x6, waiting for transfers between devices: 324 us -> 75.5 us  [the longest x1 55.3 us: local(): lax.all_gather(flat, ('ctx', 'wa'), axis=0)]
    unnamed x3 -> x0, blocking collectives: 118 us -> none
    all_gather x4 -> x1, blocking collectives: 105 us -> 38.7 us  [local(): lax.all_gather(jnp.concatenate([k_rot.reshape(row_count, kv_width), proj[...]
    all_to_all x0 -> x2, blocking collectives: none -> 58.5 us  [by_columns(): return lax.all_to_all(values, 'wa', split_axis=1, concat_axis=0, tiled=True)]
    select_n x50 -> x0, other arithmetic: 44.3 us -> none  [the longest x48 42.8 us: lap(): return jax.tree.map(lambda a, b: jnp.where(reached, a, b), new, before)]
    psum x1 -> x0, blocking collectives: 41.5 us -> none  [local(): lax.psum((g_gain_in, small_sums[0], small_sums[1], small_sums[2], small_s...]
    unnamed x19 -> x13, waiting for transfers between devices: 24.9 us -> 57.1 us
    all_to_all x0 -> x5, starting transfers between devices: none -> 25.2 us  [the longest x4 21.5 us: swap_axis(): return lax.all_to_all(parts, 'ctx', split_axis=0, concat_axis=0, tiled=True)]
  transfers between devices with their start and end apart: 22 -> 21, of which waited for: 16 -> 11; matrix products, arithmetic and copies ran while one was open for 31% -> 23% of each run, Pallas kernels for 0% -> 0%
where the time goes in v1:
time: 850 us; the launch traced here: 837 us
  waiting for transfers between devices  396 us (47%)
  local copies, waits for them, and re-layouts  99.9 us (12%)
  matrix products  97.7 us (11%)
  blocking collectives  97.2 us (11%)
  other arithmetic  90.1 us (11%)
  starting transfers between devices  37.6 us (4%)
  between operations  18.5 us (2%)
    reduce_scatter x3, waiting for transfers between devices, column_grad(): lax.psum_scatter(partial_grad.astype(jnp.bfloat16), 'ctx', scatter_dimens...  193 us
    all_to_all x2, blocking collectives, by_columns(): return lax.all_to_all(values, 'wa', split_axis=1, concat_axis=0, tiled=True)  58.5 us
    unnamed x13, waiting for transfers between devices  57.1 us
    all_gather x1, waiting for transfers between devices, local(): lax.all_gather(flat, ('ctx', 'wa'), axis=0)  55.3 us
    all_gather x1, blocking collectives, local(): lax.all_gather(jnp.concatenate([k_rot.reshape(row_count, kv_width), proj[...  38.7 us
    reduce_scatter x1, waiting for transfers between devices, local(): lax.psum_scatter(jnp.concatenate([key_grad.reshape(-1, kv_width), value_g...  32 us
    unnamed x332, local copies, waits for them, and re-layouts  28.6 us
    unnamed x26, other arithmetic  24.4 us
  transfers between devices with their start and end apart: 21, of which 11 were waited for; matrix products, arithmetic and copies ran while one was open for 23% of the time, Pallas kernels for 0%

profile of v1, /device:TPU:0, one launch (start us, length us, event | category | flops | bytes accessed | tf_op | source)
XLA Modules:
  0.0 836.7 jit_solution(10331391538475192709)
XLA Ops:
  21.7 9.3 %all-gather.7.cloned.1.call-done = bf16[512,1024]{1,0:T(8,128)(2,1)} async-done(((bf16[128,1024]{1,0:T(8,128)(2,1)}), bf16[512,1024]{1,0:T(8,128)(2,1)}) %all-gather.7.cloned.1.call-update) | async-done | bytes 1048592 | tf_op jit(solution)/shard_map/all_gather | solution.py:250
  37.8 3.7 all-to-all-start
  43.7 24.0 %all-to-all-done = bf16[4,128,1030]{1,2,0:T(8,128)(2,1)S(1)} async-done(((bf16[4,128,1030]{1,2,0:T(8,128)(2,1)}), bf16[4,128,1030]{1,2,0:T(8,128)(2,1)S(1)}, u32[]{:S(2)}, u32[]{:S(2)}) %all-to-all-start) | async-done | bytes 1054752 | tf_op jit(solution)/shard_map/all_to_all | solution.py:252
  77.5 5.1 collective-permute-start
  98.7 5.0 all-to-all-start.1
  106.9 38.7 %all_gather.22 = bf16[1024,256]{0,1:T(8,128)(2,1)S(1)} all-gather(bf16[128,256]{0,1:T(8,128)(2,1)S(1)} %pad_maximum_fusion.9), channel_id=1, replica_groups=mesh['ctx'=8,'wa'=4] {'ctx'}, dimensions={0}, use_global_device_ids=true | all-gather | bytes 589824 | tf_op jit(solution)/shard_map/all_gather | solution.py:275
  168.4 4.5 all-to-all-start.2
  180.0 5.1 fusion.208
  196.4 4.2 fusion.17
  216.3 6.1 fusion.209
  222.3 5.6 fusion.119
  240.9 3.9 fusion.72
  254.3 6.0 all-to-all-start.3
  266.5 4.1 fusion.47
  277.5 4.8 fusion.62
  292.9 6.0 all-to-all-start.4
  308.2 32.0 %reduce-scatter.9.cloned.1.call-done = bf16[128,256]{1,0:T(8,128)(2,1)} async-done(((bf16[1024,256]{1,0:T(8,128)(2,1)}), bf16[128,256]{1,0:T(8,128)(2,1)}) %reduce-scatter.9.cloned.1.call-update) | async-done | bytes 65552 | tf_op jit(solution)/shard_map/reduce_scatter | solution.py:406
  358.7 5.7 fusion.12
  386.8 18.0 %all_to_all.74 = bf16[128,4,1030]{0,2,1:T(8,128)(2,1)S(1)} all-to-all(bf16[128,4,1030]{0,2,1:T(8,128)(2,1)} %copy.613), channel_id=1, replica_groups=mesh['ctx'=8,'wa'=4] {'wa'}, dimensions={1} | all-to-all | bytes 2109440 | tf_op jit(solution)/shard_map/all_to_all | solution.py:182
  404.8 3.8 copy.646
  414.3 4.1 convolution_convert_fusion
  418.4 4.1 copy.614
  425.8 11.3 %reduce-scatter.11.cloned.1.call-done = bf16[128,1024]{1,0:T(8,128)(2,1)} async-done(((bf16[512,1024]{1,0:T(8,128)(2,1)}), bf16[128,1024]{1,0:T(8,128)(2,1)}) %reduce-scatter.11.cloned.1.call-update) | async-done | bytes 262160 | tf_op jit(solution)/shard_map/reduce_scatter | solution.py:460
  444.7 40.4 %all_to_all.75 = bf16[128,4,1536]{2,0,1:T(8,128)(2,1)} all-to-all(bf16[128,4,1536]{2,0,1:T(8,128)(2,1)S(1)} %pad_maximum_fusion), channel_id=1, replica_groups=mesh['ctx'=8,'wa'=4] {'wa'}, dimensions={1} | all-to-all | bytes 3145728 | tf_op jit(solution)/shard_map/all_to_all | solution.py:182
  485.1 10.9 %all-gather.17.cloned.1.call-done = bf16[512,5120]{1,0:T(8,128)(2,1)} async-done(((bf16[128,5120]{1,0:T(8,128)(2,1)}), bf16[512,5120]{1,0:T(8,128)(2,1)}) %all-gather.17.cloned.1.call-update) | async-done | bytes 5242896 | tf_op jit(solution)/shard_map/all_gather | solution.py:371
  503.1 4.2 convolution_convert_fusion.4
  508.4 3.8 fusion.49
  513.4 55.1 %reduce-scatter.19.cloned.1.call-done = bf16[128,1030]{1,0:T(8,128)(2,1)} async-done(((bf16[1024,1030]{1,0:T(8,128)(2,1)}), bf16[128,1030]{1,0:T(8,128)(2,1)}) %reduce-scatter.19.cloned.1.call-update) | async-done | bytes 263696
  570.5 55.3 %all-gather.15.cloned.1.call-done = f32[32,104,128]{2,1,0:T(8,128)} async-done(((f32[1,104,128]{2,1,0:T(8,128)}), f32[32,104,128]{2,1,0:T(8,128)}) %all-gather.15.cloned.1.call-update) | async-done | bytes 1703952 | tf_op jit(solution)/shard_map/all_gather | solution.py:480
  631.1 60.1 %reduce-scatter.17.cloned.1.call-done = bf16[256,256]{1,0:T(8,128)(2,1)} async-done(((bf16[2048,256]{1,0:T(8,128)(2,1)}), bf16[256,256]{1,0:T(8,128)(2,1)}) %reduce-scatter.17.cloned.1.call-update) | async-done | bytes 131088 | tf_op jit(solution)/shard_map/reduce_scatter | solution.py:200
  692.9 64.6 %reduce-scatter.13.cloned.1.call-done = bf16[256,256]{1,0:T(8,128)(2,1)} async-done(((bf16[2048,256]{1,0:T(8,128)(2,1)}), bf16[256,256]{1,0:T(8,128)(2,1)}) %reduce-scatter.13.cloned.1.call-update) | async-done | bytes 131088 | tf_op jit(solution)/shard_map/reduce_scatter | solution.py:200
  759.1 68.4 %reduce-scatter.15.cloned.1.call-done = bf16[128,1024]{1,0:T(8,128)(2,1)} async-done(((bf16[1024,1024]{1,0:T(8,128)(2,1)}), bf16[128,1024]{1,0:T(8,128)(2,1)}) %reduce-scatter.15.cloned.1.call-update) | async-done | bytes 262160 | tf_op jit(solution)/shard_map/reduce_scatter | solution.py:200
  (613 shorter events, 240.1 us)
Async XLA Ops:
  7.2 23.8 %copy-start = (bf16[1024,1030]{0,1:T(8,128)(2,1)S(1)}, bf16[1024,1030]{0,1:T(8,128)(2,1)}, u32[]{:S(2)}) copy-start(bf16[1024,1030]{0,1:T(8,128)(2,1)} %param.21) | copy-start | bytes 6328324
  7.2 23.8 %all-gather.7.cloned.1.call-start = ((), (), s32[]{:S(2)}) async-start(), calls=%async_computation.13 | async-start | bytes 1310720 | tf_op jit(solution)/shard_map/all_gather | solution.py:250
  11.4 199.8 %all-gather.9.cloned.1.call-start = ((), (), s32[]{:S(2)}) async-start(), calls=%async_computation.14 | async-start | bytes 5242880 | tf_op jit(solution)/shard_map/all_gather | solution.py:254
  12.2 204.1 %all-gather.11.cloned.1.call-start = ((), (), s32[]{:S(2)}) async-start(), calls=%async_computation.15 | async-start | bytes 10485760 | tf_op jit(solution)/shard_map/all_gather | solution.py:256
  12.9 209.4 %all-gather.13.cloned.1.call-start = ((), (), s32[]{:S(2)}) async-start(), calls=%async_computation.16 | async-start | bytes 5242880 | tf_op jit(solution)/shard_map/all_gather | solution.py:255
  18.6 65.1 %copy-start.54 = (f32[2,64]{0,1:T(8,128)}, f32[2,64]{0,1:T(8,128)S(1)}, u32[]{:S(2)}) copy-start(f32[2,64]{0,1:T(8,128)S(1)} %copy.537) | copy-start | bytes 1540
  18.6 64.2 %copy-start.149 = (f32[24]{0:T(128)}, f32[24]{0:T(128)S(1)}, u32[]{:S(2)}) copy-start(f32[24]{0:T(128)S(1)} %exp.58) | copy-start | bytes 292
  21.1 62.5 %copy-start.141 = (f32[2]{0:T(128)}, f32[2]{0:T(128)S(1)}, u32[]{:S(2)}) copy-start(f32[2]{0:T(128)S(1)} %fusion.166) | copy-start | bytes 28
  37.8 29.8 %all-to-all-start = ((bf16[4,128,1030]{1,2,0:T(8,128)(2,1)}), bf16[4,128,1030]{1,2,0:T(8,128)(2,1)S(1)}, u32[]{:S(2)}, u32[]{:S(2)}) async-start(bf16[4,128,1030]{1,2,0:T(8,128)(2,1)} %copy.524), calls=%async_computation | async-start | bytes 2113536 | tf_op jit(solution)/shard_map/all_to_all | solution.py:252
  42.2 45.2 %copy-start.83 = (f32[1792]{0:T(1024)}, f32[1792]{0:T(1024)S(1)}, u32[]{:S(2)}) copy-start(f32[1792]{0:T(1024)S(1)} %get-tuple-element.52) | copy-start | bytes 21508
  42.2 45.2 %copy-start.85 = (f32[1792]{0:T(1024)}, f32[1792]{0:T(1024)S(1)}, u32[]{:S(2)}) copy-start(f32[1792]{0:T(1024)S(1)} %get-tuple-element.53) | copy-start | bytes 21508
  43.7 63.2 %copy-start.80 = (f32[128,32]{0,1:T(8,128)}, f32[128,32]{0,1:T(8,128)S(1)}, u32[]{:S(2)}) copy-start(f32[128,32]{0,1:T(8,128)S(1)} %get-tuple-element.149) | copy-start | bytes 49156
  76.2 9.3 %collective-permute-start.1 = (bf16[1,3,1792]{2,1,0:T(4,128)(2,1)}, bf16[1,3,1792]{2,1,0:T(4,128)(2,1)}, u32[]{:S(2)}, u32[]{:S(2)}) collective-permute-start(bf16[1,3,1792]{2,1,0:T(4,128)(2,1)} %bitcast.5), channel_id=1, source_target_pairs={{4,0},{8,4},{12,8},{16,12},{20,16},{24,20},{28,24},{5,1},{9,5},{13... | collective-permute-start | bytes 32264 | tf_op jit(solution)/shard_map/ppermute | solution.py:26
  77.5 8.8 %collective-permute-start = (bf16[1,3,1792]{2,1,0:T(4,128)(2,1)}, bf16[1,3,1792]{2,1,0:T(4,128)(2,1)}, u32[]{:S(2)}, u32[]{:S(2)}) collective-permute-start(bf16[1,3,1792]{2,1,0:T(4,128)(2,1)} %bitcast.3), channel_id=1, source_target_pairs={{0,4},{4,8},{8,12},{12,16},{16,20},{20,24},{24,28},{1,5},{5,9},{9,... | collective-permute-start | bytes 32264 | tf_op jit(solution)/shard_map/ppermute | solution.py:24
  98.7 47.8 %all-to-all-start.1 = ((bf16[8,2,208,128]{3,2,1,0:T(8,128)(2,1)}), bf16[8,2,208,128]{3,2,1,0:T(8,128)(2,1)}, u32[]{:S(2)}, u32[]{:S(2)}) async-start(bf16[8,2,208,128]{3,2,1,0:T(8,128)(2,1)} %pad_maximum_fusion.2), calls=%async_computation.1 | async-start | bytes 1703936 | tf_op jit(solution)/shard_map/all_to_all | solution.py:153
  148.4 17.9 %copy-start.97 = (f32[1,192]{1,0:T(1,128)}, f32[1,192]{1,0:T(1,128)S(1)}, u32[]{:S(2)}) copy-start(f32[1,192]{1,0:T(1,128)S(1)} %get-tuple-element.121) | copy-start | bytes 2308
  168.4 23.2 %all-to-all-start.2 = ((bf16[8,2,192,128]{3,2,1,0:T(8,128)(2,1)}), bf16[8,2,192,128]{3,2,1,0:T(8,128)(2,1)}, u32[]{:S(2)}, u32[]{:S(2)}) async-start(bf16[8,2,192,128]{3,2,1,0:T(8,128)(2,1)} %copy.543), calls=%async_computation.2 | async-start | bytes 1572864 | tf_op jit(solution)/shard_map/all_to_all | solution.py:153
  254.3 28.1 %all-to-all-start.3 = ((bf16[8,2,192,128]{3,2,1,0:T(8,128)(2,1)}), bf16[8,2,192,128]{3,2,1,0:T(8,128)(2,1)}, u32[]{:S(2)}, u32[]{:S(2)}) async-start(bf16[8,2,192,128]{3,2,1,0:T(8,128)(2,1)} %copy_bitcast_fusion.2), calls=%async_computation.3 | async-start | bytes 1572864 | tf_op jit(solution)/shard_map/all_to_all | solution.py:153
  260.3 79.9 %reduce-scatter.9.cloned.1.call-start = ((), (), s32[]{:S(2)}) async-start(), calls=%async_computation.17 | async-start | bytes 589824 | tf_op jit(solution)/shard_map/reduce_scatter | solution.py:406
  282.3 24.2 %copy-start.66 = (f32[2,64,64]{2,1,0:T(8,128)}, f32[2,64,64]{2,1,0:T(8,128)S(1)}, u32[]{:S(2)}) copy-start(f32[2,64,64]{2,1,0:T(8,128)S(1)} %get-tuple-element.46) | copy-start | bytes 98308
  292.9 49.6 %all-to-all-start.4 = ((bf16[8,2,192,128]{3,2,1,0:T(8,128)(2,1)}), bf16[8,2,192,128]{3,2,1,0:T(8,128)(2,1)}, u32[]{:S(2)}, u32[]{:S(2)}) async-start(bf16[8,2,192,128]{3,2,1,0:T(8,128)(2,1)} %copy.559), calls=%async_computation.4 | async-start | bytes 1572864 | tf_op jit(solution)/shard_map/all_to_all | solution.py:153
  298.9 138.2 %reduce-scatter.11.cloned.1.call-start = ((), (), s32[]{:S(2)}) async-start(), calls=%async_computation.18 | async-start | bytes 1310720 | tf_op jit(solution)/shard_map/reduce_scatter | solution.py:460
  302.8 38.9 %copy-start.79 = (f32[128,32]{0,1:T(8,128)S(1)}, f32[128,32]{0,1:T(8,128)}, u32[]{:S(2)}) copy-start(f32[128,32]{0,1:T(8,128)} %get-tuple-element.148) | copy-start | bytes 49156
  371.0 6.4 collective-permute-start.2
  374.2 5.7 collective-permute-start.3
  412.9 83.1 %all-gather.17.cloned.1.call-start = ((), (), s32[]{:S(2)}) async-start(), calls=%async_computation.20 | async-start | bytes 6553600 | tf_op jit(solution)/shard_map/all_gather | solution.py:371
  414.2 154.3 %reduce-scatter.19.cloned.1.call-start = ((), (), s32[]{:S(2)}) async-start(), calls=%async_computation.24 | async-start | bytes 2654208
  422.6 203.2 %all-gather.15.cloned.1.call-start = ((), (), s32[]{:S(2)}) async-start(), calls=%async_computation.19 | async-start | bytes 1757184 | tf_op jit(solution)/shard_map/all_gather | solution.py:480
  425.1 19.4 %copy-start.17 = (bf16[128,4096]{1,0:T(8,128)(2,1)S(1)}, bf16[128,4096]{1,0:T(8,128)(2,1)}, u32[]{:S(2)}) copy-start(bf16[128,4096]{1,0:T(8,128)(2,1)} %copy-done.16) | copy-start | bytes 3145732
  439.8 251.5 %reduce-scatter.17.cloned.1.call-start = ((), (), s32[]{:S(2)}) async-start(), calls=%async_computation.23 | async-start | bytes 1179648 | tf_op jit(solution)/shard_map/reduce_scatter | solution.py:200
  499.3 258.1 %reduce-scatter.13.cloned.1.call-start = ((), (), s32[]{:S(2)}) async-start(), calls=%async_computation.21 | async-start | bytes 1179648 | tf_op jit(solution)/shard_map/reduce_scatter | solution.py:200
  502.7 324.8 %reduce-scatter.15.cloned.1.call-start = ((), (), s32[]{:S(2)}) async-start(), calls=%async_computation.22 | async-start | bytes 2359296 | tf_op jit(solution)/shard_map/reduce_scatter | solution.py:200
  (151 other events, 767.1 us)
Sparse Core Ops, SparseCore 0:
  11.5 19.4 all-gather.6
  32.5 46.3 all-gather.8
  80.5 58.2 all-gather.10
  140.2 35.0 all-gather.12
  274.5 65.6 reduce-scatter.8
  413.0 24.0 reduce-scatter.10
  438.7 57.2 all-gather.16
  499.5 68.9 reduce-scatter.18
  571.4 54.3 all-gather.14
  629.0 62.1 reduce-scatter.16
  695.0 62.3 reduce-scatter.12
  760.9 66.6 reduce-scatter.14
